TPU v7x, 32 devices: a whole 2x2x4 slice. The times are simulated.
32 devices in a mesh: seq: 4 (over x, core), head: 4 (over z), batch: 2 (over y).
Axes of the slice: x: 2, y: 2, z: 4, core: 2. Of those that a mesh axis runs over, the one named last changes fastest.
Arguments:
- hyena_inputs: bfloat16 [4096, 3, 8192], P(('batch', 'seq'), None, 'head'), parts along dimension 0, may hold values from -6 to 6
- short_filter: float32 [3, 3, 8192], P(None, None, 'head'), may hold values from -3.5 to 3.5
- medium_filter: float32 [128, 8192], P(None, 'head'), may hold values from -0.5 to 0.5
- q_proj: bfloat16 [4096, 8192], P(('batch', 'seq'), 'head'), parts along dimension 0, may hold values from -8 to 8
- k_proj: bfloat16 [4096, 8192], P(('batch', 'seq'), 'head'), parts along dimension 0, may hold values from -8 to 8
- out_weight: bfloat16 [8192, 8192], P('head'), may hold values from -0.25 to 0.25
Outputs:
- hyena_out: bfloat16 [4096, 8192], P(('batch', 'seq'), 'head'), parts along dimension 0
- mixed: bfloat16 [4096, 8192], P(('batch', 'seq'), 'head'), parts along dimension 0
There are 2 independent parts, one for each index of `batch`. A program takes and returns all parts, laid end to end along the dimension named above; an argument that names none is the same for every part. Nothing has to cross between parts.
All inputs are finite; a program needn't handle non-finite values.
Results may differ from a plain program's by a relative error of at most 0.011.
Values may be sent and summed in bfloat16 or wider, within the bound.
A program may use at most 192 MiB of HBM per device.

v0:
```python
import math
import jax
import jax.numpy as jnp
from jax import lax
from jax.sharding import PartitionSpec as P

HEAD_SIZE = 128


def passed_along(x, axis, by):
    length = lax.axis_size(axis)
    pairs = [(i, i + by) for i in range(length) if 0 <= i + by < length]
    return lax.ppermute(x, axis, pairs)


def causal_depthwise(extended, taps, out_rows):
    tap_count = taps.shape[0]
    window = extended[extended.shape[0] - out_rows - tap_count + 1 :]
    kernel = taps[::-1][:, None, :]
    result = lax.conv_general_dilated(
        window[None],
        kernel,
        (1,),
        "VALID",
        feature_group_count=extended.shape[1],
        dimension_numbers=("NWC", "WIO", "NWC"),
        precision=lax.Precision.HIGHEST,
    )
    return result[0]


def per_device(hyena_inputs, short_filter, medium_filter, q_proj, k_proj, out_weight):
    tok_rows = hyena_inputs.shape[0]
    chan_width = hyena_inputs.shape[2]
    short_taps = short_filter.shape[1]
    med_taps = medium_filter.shape[0]
    short_table = jnp.transpose(short_filter, (1, 0, 2)).reshape(short_taps, 3 * chan_width)
    input_margin = passed_along(hyena_inputs[tok_rows - (short_taps - 1) :], "seq", 1)
    joined = (
        jnp.concatenate([input_margin, hyena_inputs], 0)
        .astype(jnp.float32)
        .reshape(-1, 3 * chan_width)
    )
    filtered = causal_depthwise(joined, short_table, tok_rows).reshape(tok_rows, 3, chan_width)
    product = (filtered[:, 1] * filtered[:, 2]).astype(jnp.bfloat16)
    product_margin = passed_along(product[tok_rows - (med_taps - 1) :], "seq", 1)
    product_ext = jnp.concatenate([product_margin, product], 0)
    medium = causal_depthwise(product_ext.astype(jnp.float32), medium_filter, tok_rows)
    hyena_out = (filtered[:, 0] * medium).astype(jnp.bfloat16)
    head_count = chan_width // HEAD_SIZE
    score_scale = HEAD_SIZE ** (-0.5)
    seq_index = lax.axis_index("seq")
    queries = q_proj.reshape(tok_rows, head_count, HEAD_SIZE)
    query_pos = seq_index * tok_rows + jnp.arange(tok_rows, dtype=jnp.int32)
    last_query = seq_index * tok_rows + tok_rows - 1
    initial = (
        jnp.zeros((head_count, tok_rows, HEAD_SIZE), jnp.float32),
        jnp.full((head_count, tok_rows), -1e30, jnp.float32),
        jnp.zeros((head_count, tok_rows), jnp.float32),
    )
    carried = initial
    first_row = jnp.int32(0)
    key_piece = lax.all_gather(k_proj, "seq", axis=0, tiled=True)
    value_piece = lax.all_gather(hyena_out, "seq", axis=0, tiled=True)
    piece_rows = key_piece.shape[0]
    block_rows = math.gcd(piece_rows, 512)
    block_count = piece_rows // block_rows
    key_blocks = key_piece.reshape(block_count, block_rows, head_count, HEAD_SIZE)
    value_blocks = value_piece.reshape(block_count, block_rows, head_count, HEAD_SIZE)

    def visit(running, block_item):
        key_blk, value_blk, block_number = block_item
        key_start = first_row + block_number * block_rows

        def attend(current):
            weighted, run_max, total_sum = current
            scores = (
                jnp.einsum("qhd,khd->hqk", queries, key_blk, preferred_element_type=jnp.float32)
                * score_scale
            )
            key_pos = key_start + jnp.arange(block_rows, dtype=jnp.int32)
            allowed = key_pos[None, None, :] <= query_pos[None, :, None]
            masked = jnp.where(allowed, scores, -jnp.inf)
            new_max = jnp.maximum(run_max, jnp.max(masked, axis=-1))
            weights = jnp.exp(masked - new_max[..., None])
            factor = jnp.exp(run_max - new_max)
            new_total = total_sum * factor + jnp.sum(weights, axis=-1)
            new_weighted = weighted * factor[..., None] + jnp.einsum(
                "hqk,khd->hqd",
                weights.astype(jnp.bfloat16),
                value_blk,
                preferred_element_type=jnp.float32,
            )
            return (new_weighted, new_max, new_total)

        def keep_state(current):
            return current

        return (lax.cond(key_start <= last_query, attend, keep_state, running), None)

    carried, unused = lax.scan(
        visit, carried, (key_blocks, value_blocks, jnp.arange(block_count, dtype=jnp.int32))
    )
    weighted, run_max, total_sum = carried
    attended = (
        (weighted / total_sum[..., None])
        .transpose(1, 0, 2)
        .reshape(tok_rows, chan_width)
        .astype(jnp.bfloat16)
    )
    summed = lax.psum_scatter(
        lax.dot_general(
            out_weight, attended, (((0,), (1,)), ((), ())), preferred_element_type=jnp.float32
        ).astype(jnp.bfloat16),
        "head",
        scatter_dimension=0,
        tiled=True,
    ).astype(jnp.float32)
    return (hyena_out, summed.T.astype(jnp.bfloat16))


def solution(mesh):
    return jax.shard_map(
        per_device,
        mesh=mesh,
        in_specs=(
            P(("batch", "seq"), None, "head"),
            P(None, None, "head"),
            P(None, "head"),
            P(("batch", "seq"), "head"),
            P(("batch", "seq"), "head"),
            P("head", None),
        ),
        out_specs=(P(("batch", "seq"), "head"), P(("batch", "seq"), "head")),
        check_vma=False,
    )
```

profile of v0, /device:TPU:0, one launch (start us, length us, event | category | flops | bytes accessed | tf_op | source)
XLA Modules:
  0.0 636.0 jit_solution(6922452532543686896)
XLA Ops:
  10.6 16.9 %rev.6 = f32[3,6144]{1,0:T(4,128)S(1)} reverse(f32[3,6144]{1,0:T(4,128)} %bitcast.76), dimensions={0} | reverse | bytes 147456 | tf_op jit(solution)/shard_map/rev | solution.py:19
  27.6 7.8 %pad_maximum_fusion = bf16[514,3,2048]{2,0,1:T(8,128)(2,1)} fusion(bf16[512,3,2048]{2,0,1:T(8,128)(2,1)} %param.10, bf16[2,3,2048]{2,0,1:T(2,128)(2,1)S(1)} %collective-permute-done), kind=kLoop, calls=%fused_computation.37 | loop fusion | flops 12632064 | bytes 12632064 | tf_op jit(solution)/shard_map/concatenate | solution.py:40
  35.4 9.7 %copy.12 = bf16[514,3,2048]{0,2,1:T(8,128)(2,1)} copy(bf16[514,3,2048]{2,0,1:T(8,128)(2,1)} %pad_maximum_fusion) | data formatting | bytes 12632064 | tf_op jit(solution)/shard_map/concatenate | solution.py:40
  52.1 20.5 %reshape.76 = bf16[1,8,65,6144]{2,1,3,0:T(8,128)(2,1)} reshape(bf16[1,520,6144]{1,2,0:T(8,128)(2,1)} %pad) | data formatting | bytes 12779520 | tf_op jit(solution)/shard_map/conv_general_dilated | solution.py:20
  72.7 16.8 %copy.15 = bf16[1,8,65,6144]{3,1,2,0:T(8,128)(2,1)} copy(bf16[1,8,65,6144]{2,1,3,0:T(8,128)(2,1)} %reshape.76) | data formatting | bytes 12779520 | tf_op jit(solution)/shard_map/conv_general_dilated | solution.py:20
  90.4 11.8 %fusion.30 = f32[8,65,6144]{2,0,1:T(8,128)} fusion(f32[3,1,6144]{2,1,0:T(1,128)S(1)} %broadcast_in_dim.40, bf16[1,7,2,6144]{3,1,2,0:T(8,128)(2,1)S(1)} %slice.26, bf16[1,8,65,6144]{3,1,2,0:T(8,128)(2,1)} %copy.15, pred[8,65]{0,1:T(8,128)(4,1)S(1)} %copy-done.4), kind=kOutput, calls=%fused_computation.33 | convolution fusion | flops 137969664 | bytes 19415560 | tf_op jit(solution)/shard_map/conv_general_dilated | solution.py:20
  102.2 17.2 %copy.16 = f32[8,65,6144]{2,1,0:T(8,128)} copy(f32[8,65,6144]{2,0,1:T(8,128)} %fusion.30) | data formatting | bytes 25559040 | tf_op jit(solution)/shard_map/conv_general_dilated | solution.py:20
  119.4 11.3 %reshape.72 = f32[1,520,6144]{2,1,0:T(8,128)} reshape(f32[8,65,6144]{2,1,0:T(8,128)} %copy.16) | data formatting | bytes 25559040 | tf_op jit(solution)/shard_map/conv_general_dilated | solution.py:20
  130.7 10.6 %slice.27 = f32[1,512,6144]{2,1,0:T(8,128)} slice(f32[1,520,6144]{2,1,0:T(8,128)} %reshape.72), slice={[0:1], [0:512], [0:6144]} | slice | bytes 25165824 | tf_op jit(solution)/shard_map/conv_general_dilated | solution.py:20
  141.3 12.8 %copy.17 = f32[1,512,6144]{1,2,0:T(8,128)} copy(f32[1,512,6144]{2,1,0:T(8,128)} %slice.27) | data formatting | bytes 25165824 | tf_op jit(solution)/shard_map/conv_general_dilated | solution.py:20
  182.8 11.5 %copy.20 = bf16[1,639,2048]{2,0,1:T(2,128)(2,1)} copy(bf16[1,639,2048]{1,2,0:T(8,128)(2,1)} %maximum_bitcast_fusion) | data formatting | bytes 5234688 | tf_op jit(solution)/shard_map/broadcast_in_dim | solution.py:21
  194.4 48.5 %fusion.39 = f32[1,512,2048]{2,0,1:T(1,128)S(1)} fusion(bf16[1,639,2048]{2,0,1:T(2,128)(2,1)} %copy.20, f32[128,1,2048]{2,0,1:T(8,128)S(1)} %bitcast.75), kind=kOutput, calls=%fused_computation.45 | convolution fusion | flops 1610612736 | bytes 7860224 | tf_op jit(solution)/shard_map/conv_general_dilated | solution.py:20
  251.5 10.9 %copy.34 = bf16[256,8,16,128]{3,2,1,0:T(8,128)(2,1)} copy(bf16[256,8,16,128]{3,1,2,0:T(8,128)(2,1)} %bitcast.71) | data formatting | bytes 16777216
  262.3 8.8 %copy.23 = bf16[4,512,16,128]{3,1,2,0:T(8,128)(2,1)} copy(bf16[4,512,16,128]{3,2,1,0:T(8,128)(2,1)} %bitcast.67) | data formatting | bytes 16777216
  271.2 33.2 %all-gather.5.cloned.1.call-done = bf16[2048,2048]{1,0:T(8,128)(2,1)} async-done(((bf16[512,2048]{1,0:T(8,128)(2,1)}), bf16[2048,2048]{1,0:T(8,128)(2,1)}) %all-gather.5.cloned.1.call-update) | async-done | bytes 8388624 | tf_op jit(solution)/shard_map/all_gather | solution.py:64
  304.4 9.8 %copy.35 = bf16[256,8,16,128]{3,2,1,0:T(8,128)(2,1)} copy(bf16[256,8,16,128]{3,1,2,0:T(8,128)(2,1)} %bitcast.72) | data formatting | bytes 16777216
  314.1 8.8 %copy.25 = bf16[4,512,16,128]{3,1,2,0:T(8,128)(2,1)} copy(bf16[4,512,16,128]{3,2,1,0:T(8,128)(2,1)} %bitcast.68) | data formatting | bytes 16777216
  325.4 35.2 %while.15 = (s32[]{:T(128)}, f32[16,512,128]{2,1,0:T(8,128)}, f32[16,512]{1,0:T(8,128)S(1)}, f32[16,512]{1,0:T(8,128)S(1)}, s32[4]{0:T(128)S(1)}, /*index=5*/s32...) while((s32[]{:T(128)}, f32[16,512,128]{2,1,0:T(8,128)}, ...), condition=%wide.region_5.6_spmd.clone, body=%wide.region_0.5_spmd.clone.sunk | while | flops 2195997696 | bytes 66598184 | solution.py:101
  326.9 30.0 %conditional.3 = ((f32[16,512,128]{2,1,0:T(8,128)}, f32[16,512]{1,0:T(8,128)S(1)}, f32[16,512]{1,0:T(8,128)S(1)})) conditional(s32[]{:T(128)} %convert_element_type.60, (f32[16,512,128]{2,1,0:T(8,128)}, f32[16,512]{1,0:T(8,128)S(1)}, f32[16,512]{1,0:T(8,128)S(1)}) %tuple.46, (s32[]{:T(128)}, s32[]{:T(128)}, bf16[4,512,16,128]{3,1,2,0:T(8,128)(2,1)}, ...), branch_computations={%region_1.1_spmd, %region_2.4_spmd} | conditional | flops 2195997696 | bytes 66595880 | solution.py:99
  327.1 8.8 %fusion.4 = (f32[16,512]{1,0:T(8,128)S(1)}, f32[16,512,512]{2,1,0:T(8,128)}) fusion(pred[512,512]{0,1:T(8,128)(4,1)S(1)} %broadcast_compare_fusion, bf16[512,16,128]{2,0,1:T(8,128)(2,1)S(1)} %get-tuple-element.117, bf16[4,512,16,128]{3,1,2,0:T(8,128)(2,1)} %get-tuple-element.115, s32[]{:T(128)} %get-tuple-element.116), kind=kOutput, calls=%fused_computation.5 | convolution fusion | flops 1086316544 | bytes 21266944 | tf_op jit(solution)/shard_map/while/body/eval_jaxpr/cond/branch_1_fun/qhd,khd->hqk/dot_general | solution.py:78
  335.9 9.1 %fusion.2 = f32[16,512]{1,0:T(8,128)S(1)} fusion(f32[16,512,512]{2,1,0:T(8,128)} %get-tuple-element.212, f32[16,512]{1,0:T(8,128)S(1)} %max.4, pred[512,512]{0,1:T(8,128)(4,1)S(1)} %broadcast_compare_fusion), kind=kLoop, calls=%fused_computation.3 | loop fusion | flops 16769024 | bytes 17104896 | tf_op jit(solution)/shard_map/while/body/eval_jaxpr/cond/branch_1_fun/reduce_sum | solution.py:87
  345.1 11.7 %multiply_add_fusion = f32[16,512,128]{2,1,0:T(8,128)} fusion(f32[16,512,128]{2,1,0:T(8,128)} %get-tuple-element.111, f32[16,512]{1,0:T(8,128)S(1)} %get-tuple-element.210, bf16[4,512,16,128]{3,1,2,0:T(8,128)(2,1)} %get-tuple-element.118, s32[]{:T(128)} %get-tuple-element.116, f32[16,512,512]{2,1,0:T(8,128)} %get-tuple-element.212, f32[16,512]{1,0:T(8,128)S(1)} %max.4, ...), kind=kOutput, calls=%fused_computation.11 | convolution fusion | flops 1092616192 | bytes 27591168 | tf_op jit(solution)/shard_map/while/body/eval_jaxpr/cond/branch_1_fun/hqk,khd->hqd/dot_general | solution.py:88
  368.8 26.1 %fusion.25 = bf16[8192,512]{0,1:T(8,128)(2,1)} fusion(bf16[512,2048]{0,1:T(8,128)(2,1)S(1)} %bitcast.74, bf16[2048,8192]{1,0:T(8,128)(2,1)} %param.15), kind=kOutput, calls=%fused_computation.29 | convolution fusion | flops 17184063488 | bytes 44040192 | tf_op jit(solution)/shard_map/dot_general | solution.py:112
  395.0 234.0 %reduce-scatter.2.cloned.1.call-done = bf16[2048,512]{0,1:T(8,128)(2,1)} async-done(((bf16[8192,512]{0,1:T(8,128)(2,1)}), bf16[2048,512]{0,1:T(8,128)(2,1)}) %reduce-scatter.2.cloned.1.call-update) | async-done | bytes 2097168 | tf_op jit(solution)/shard_map/reduce_scatter | solution.py:111
  (55 shorter events, 62.1 us)
Async XLA Ops:
  7.2 244.3 %all-gather.3.cloned.1.call-start = ((), (), s32[]{:S(2)}) async-start(), calls=%async_computation.1 | async-start | bytes 10485760 | tf_op jit(solution)/shard_map/all_gather | solution.py:63
  8.1 19.4 %collective-permute-start = (bf16[2,3,2048]{2,0,1:T(2,128)(2,1)S(1)}, bf16[2,3,2048]{2,0,1:T(2,128)(2,1)S(1)}, u32[]{:S(2)}, u32[]{:S(2)}) collective-permute-start(bf16[2,3,2048]{2,0,1:T(2,128)(2,1)S(1)} %slice.18), channel_id=1, source_target_pairs={{0,8},{8,16},{16,24},{1,9},{9,17},{17,25},{2,10},{10,18},{18,26},{... | collective-permute-start | bytes 73736 | tf_op jit(solution)/shard_map/ppermute | solution.py:13
  10.5 293.8 %all-gather.5.cloned.1.call-start = ((), (), s32[]{:S(2)}) async-start(), calls=%async_computation.2 | async-start | bytes 10485760 | tf_op jit(solution)/shard_map/all_gather | solution.py:64
  72.7 17.8 %copy-start.4 = (pred[8,65]{0,1:T(8,128)(4,1)S(1)}, pred[8,65]{0,1:T(8,128)(4,1)}, u32[]{:S(2)}) copy-start(pred[8,65]{0,1:T(8,128)(4,1)} %constant.55) | copy-start | bytes 1564
  154.0 14.1 %copy-start.2 = (f32[128,2048]{1,0:T(8,128)S(1)}, f32[128,2048]{1,0:T(8,128)}, u32[]{:S(2)}) copy-start(f32[128,2048]{1,0:T(8,128)} %param.12) | copy-start | bytes 3145732
  162.8 16.0 %collective-permute-start.1 = (bf16[127,2048]{0,1:T(8,128)(2,1)}, bf16[127,2048]{0,1:T(8,128)(2,1)}, u32[]{:S(2)}, u32[]{:S(2)}) collective-permute-start(bf16[127,2048]{0,1:T(8,128)(2,1)} %slice_bitcast_fusion), channel_id=1, source_target_pairs={{0,8},{8,16},{16,24},{1,9},{9,17},{17,25},{2,10},{10,18},{18,26},{... | collective-permute-start | bytes 1560584 | tf_op jit(solution)/shard_map/ppermute | solution.py:13
  178.8 15.6 %copy-start.3 = (f32[128,2048]{1,0:T(8,128)S(1)}, f32[128,2048]{1,0:T(8,128)}, u32[]{:S(2)}) copy-start(f32[128,2048]{1,0:T(8,128)} %rev.7) | copy-start | bytes 3145732
  194.4 48.5 %copy-start = (f32[512,1,2048]{2,0,1:T(8,128)S(1)}, f32[512,1,2048]{2,0,1:T(8,128)}, u32[]{:S(2)}) copy-start(f32[512,1,2048]{2,0,1:T(8,128)} %copy.33) | copy-start | bytes 12582916
  242.9 2.8 copy-start.1
  245.6 383.4 %reduce-scatter.2.cloned.1.call-start = ((), (), s32[]{:S(2)}) async-start(), calls=%async_computation.3 | async-start | bytes 10485760 | tf_op jit(solution)/shard_map/reduce_scatter | solution.py:111
Sparse Core Ops, SparseCore 0:
  10.6 60.8 all-gather.2
  245.7 58.5 all-gather.4
  395.1 233.8 reduce-scatter.1
where the time goes:
time: 644 us; the launch traced here: 636 us
  waiting for transfers between devices  267 us (41%)
  local copies, waits for them, and re-layouts  202 us (31%)
  matrix products  107 us (17%)
  other arithmetic  34.5 us (5%)
  between operations  14.4 us (2%)
  starting transfers between devices  7.87 us (1%)
    reduce_scatter x1, waiting for transfers between devices, per_device(): lax.psum_scatter(lax.dot_general(out_weight, attended, (((0,), (1,)), (()...  234 us
    conv_general_dilated x7, local copies, waits for them, and re-layouts, causal_depthwise(): lax.conv_general_dilated(window[None], kernel, (1,), 'VALID', feature_gro...  90.1 us
    conv_general_dilated x2, matrix products, causal_depthwise(): lax.conv_general_dilated(window[None], kernel, (1,), 'VALID', feature_gro...  60.3 us
    unnamed x17, local copies, waits for them, and re-layouts  49.5 us
    all_gather x1, waiting for transfers between devices, per_device(): value_piece = lax.all_gather(hyena_out, 'seq', axis=0, tiled=True)  33.2 us
    dot_general x1, matrix products, per_device(): lax.dot_general(out_weight, attended, (((0,), (1,)), ((), ())), preferred...  26.1 us
    rev x2, local copies, waits for them, and re-layouts, causal_depthwise(): kernel = taps[::-1][:, None, :]  22.1 us
  transfers between devices with their start and end apart: 5, of which 2 were waited for; matrix products, arithmetic and copies ran while one was open for 40% of the time, Pallas kernels for 0%

commit v1 on v0

--- a/solution.py
+++ b/solution.py
@@ -61,7 +61,15 @@
     carried = initial
     first_row = jnp.int32(0)
     key_piece = lax.all_gather(k_proj, "seq", axis=0, tiled=True)
-    value_piece = lax.all_gather(hyena_out, "seq", axis=0, tiled=True)
+    ways, here = (lax.axis_size("seq"), lax.axis_index("seq"))
+    grown, reach = (hyena_out, 1)
+    while reach < ways:
+        theirs = lax.ppermute(grown, "seq", [(d, d ^ reach) for d in range(ways)])
+        mine_first = jnp.concatenate([grown, theirs], axis=0)
+        theirs_first = jnp.concatenate([theirs, grown], axis=0)
+        grown = jnp.where(here & reach == 0, mine_first, theirs_first)
+        reach = 2 * reach
+    value_piece = grown
     piece_rows = key_piece.shape[0]
     block_rows = math.gcd(piece_rows, 512)
     block_count = piece_rows // block_rows

time: 644 us -> 715 us (1.11)
  waiting for transfers between devices: 267 us -> 324 us
  other arithmetic: 34.5 us -> 49.8 us
    ppermute x0 -> x2, waiting for transfers between devices: none -> 90.2 us  [per_device(): theirs = lax.ppermute(grown, 'seq', [(d, d ^ reach) for d in range(ways)])]
    all_gather x1 -> x0, waiting for transfers between devices: 33.2 us -> none  [per_device(): value_piece = lax.all_gather(hyena_out, 'seq', axis=0, tiled=True)]
    unnamed x0 -> x1, other arithmetic: none -> 10.2 us
  transfers between devices with their start and end apart: 5 -> 6, of which waited for: 2 -> 3; matrix products, arithmetic and copies ran while one was open for 40% -> 19% of each run, Pallas kernels for 0% -> 0%
where the time goes in v1:
time: 715 us; the launch traced here: 707 us
  waiting for transfers between devices  324 us (45%)
  local copies, waits for them, and re-layouts  202 us (28%)
  matrix products  106 us (15%)
  other arithmetic  49.8 us (7%)
  between operations  14.4 us (2%)
  starting transfers between devices  7.83 us (1%)
    reduce_scatter x1, waiting for transfers between devices, per_device(): lax.psum_scatter(lax.dot_general(out_weight, attended, (((0,), (1,)), (()...  233 us
    ppermute x2, waiting for transfers between devices, per_device(): theirs = lax.ppermute(grown, 'seq', [(d, d ^ reach) for d in range(ways)])  90.2 us
    conv_general_dilated x7, local copies, waits for them, and re-layouts, causal_depthwise(): lax.conv_general_dilated(window[None], kernel, (1,), 'VALID', feature_gro...  90.1 us
    conv_general_dilated x2, matrix products, causal_depthwise(): lax.conv_general_dilated(window[None], kernel, (1,), 'VALID', feature_gro...  60 us
    unnamed x17, local copies, waits for them, and re-layouts  49.8 us
    dot_general x1, matrix products, per_device(): lax.dot_general(out_weight, attended, (((0,), (1,)), ((), ())), preferred...  26 us
    rev x2, local copies, waits for them, and re-layouts, causal_depthwise(): kernel = taps[::-1][:, None, :]  22 us
  transfers between devices with their start and end apart: 6, of which 3 were waited for; matrix products, arithmetic and copies ran while one was open for 19% of the time, Pallas kernels for 0%

profile of v1, /device:TPU:0, one launch (start us, length us, event | category | flops | bytes accessed | tf_op | source)
XLA Modules:
  0.0 707.3 jit_solution(401534202147556825)
XLA Ops:
  10.5 16.9 %rev.6 = f32[3,6144]{1,0:T(4,128)S(1)} reverse(f32[3,6144]{1,0:T(4,128)} %bitcast.76), dimensions={0} | reverse | bytes 147456 | tf_op jit(solution)/shard_map/rev | solution.py:19
  35.3 9.7 %copy.12 = bf16[514,3,2048]{0,2,1:T(8,128)(2,1)} copy(bf16[514,3,2048]{2,0,1:T(8,128)(2,1)} %pad_maximum_fusion) | data formatting | bytes 12632064 | tf_op jit(solution)/shard_map/concatenate | solution.py:40
  52.0 20.5 %reshape.77 = bf16[1,8,65,6144]{2,1,3,0:T(8,128)(2,1)} reshape(bf16[1,520,6144]{1,2,0:T(8,128)(2,1)} %pad) | data formatting | bytes 12779520 | tf_op jit(solution)/shard_map/conv_general_dilated | solution.py:20
  72.5 16.8 %copy.15 = bf16[1,8,65,6144]{3,1,2,0:T(8,128)(2,1)} copy(bf16[1,8,65,6144]{2,1,3,0:T(8,128)(2,1)} %reshape.77) | data formatting | bytes 12779520 | tf_op jit(solution)/shard_map/conv_general_dilated | solution.py:20
  90.3 11.5 %fusion.31 = f32[8,65,6144]{2,0,1:T(8,128)} fusion(f32[3,1,6144]{2,1,0:T(1,128)S(1)} %broadcast_in_dim.40, bf16[1,7,2,6144]{3,1,2,0:T(8,128)(2,1)S(1)} %slice.26, bf16[1,8,65,6144]{3,1,2,0:T(8,128)(2,1)} %copy.15, pred[8,65]{0,1:T(8,128)(4,1)S(1)} %copy-done.4), kind=kOutput, calls=%fused_computation.35 | convolution fusion | flops 137969664 | bytes 19415560 | tf_op jit(solution)/shard_map/conv_general_dilated | solution.py:20
  101.9 17.2 %copy.16 = f32[8,65,6144]{2,1,0:T(8,128)} copy(f32[8,65,6144]{2,0,1:T(8,128)} %fusion.31) | data formatting | bytes 25559040 | tf_op jit(solution)/shard_map/conv_general_dilated | solution.py:20
  119.1 11.2 %reshape.73 = f32[1,520,6144]{2,1,0:T(8,128)} reshape(f32[8,65,6144]{2,1,0:T(8,128)} %copy.16) | data formatting | bytes 25559040 | tf_op jit(solution)/shard_map/conv_general_dilated | solution.py:20
  130.3 10.6 %slice.27 = f32[1,512,6144]{2,1,0:T(8,128)} slice(f32[1,520,6144]{2,1,0:T(8,128)} %reshape.73), slice={[0:1], [0:512], [0:6144]} | slice | bytes 25165824 | tf_op jit(solution)/shard_map/conv_general_dilated | solution.py:20
  140.9 12.8 %copy.17 = f32[1,512,6144]{1,2,0:T(8,128)} copy(f32[1,512,6144]{2,1,0:T(8,128)} %slice.27) | data formatting | bytes 25165824 | tf_op jit(solution)/shard_map/conv_general_dilated | solution.py:20
  183.1 11.5 %copy.20 = bf16[1,639,2048]{2,0,1:T(2,128)(2,1)} copy(bf16[1,639,2048]{1,2,0:T(8,128)(2,1)} %maximum_bitcast_fusion) | data formatting | bytes 5234688 | tf_op jit(solution)/shard_map/broadcast_in_dim | solution.py:21
  194.6 48.5 %fusion.40 = f32[1,512,2048]{2,0,1:T(1,128)S(1)} fusion(bf16[1,639,2048]{2,0,1:T(2,128)(2,1)} %copy.20, f32[128,1,2048]{2,0,1:T(8,128)S(1)} %bitcast.75), kind=kOutput, calls=%fused_computation.48 | convolution fusion | flops 1610612736 | bytes 7860224 | tf_op jit(solution)/shard_map/conv_general_dilated | solution.py:20
  262.1 86.0 %collective-permute-done.3 = bf16[1024,2048]{1,0:T(8,128)(2,1)} collective-permute-done((bf16[1024,2048]{1,0:T(8,128)(2,1)}, bf16[1024,2048]{1,0:T(8,128)(2,1)}, u32[]{:S(2)}, u32[]{:S(2)}) %collective-permute-start.3) | collective-permute-done | bytes 4194336 | tf_op jit(solution)/shard_map/ppermute | solution.py:67
  348.0 10.2 %fusion.26 = bf16[256,8,16,128]{3,1,2,0:T(8,128)(2,1)} fusion(bf16[1024,2048]{1,0:T(8,128)(2,1)} %collective-permute-done.3, bf16[1024,2048]{1,0:T(8,128)(2,1)} %maximum_select_fusion.1, pred[]{:T(512)S(6)} %eq.6), kind=kLoop, calls=%fused_computation.31 | loop fusion | flops 37748736 | bytes 16777216
  358.3 9.8 %copy.35 = bf16[256,8,16,128]{3,2,1,0:T(8,128)(2,1)} copy(bf16[256,8,16,128]{3,1,2,0:T(8,128)(2,1)} %fusion.26) | data formatting | bytes 16777216
  368.0 8.8 %copy.25 = bf16[4,512,16,128]{3,1,2,0:T(8,128)(2,1)} copy(bf16[4,512,16,128]{3,2,1,0:T(8,128)(2,1)} %bitcast.68) | data formatting | bytes 16777216
  376.8 9.8 %copy.34 = bf16[256,8,16,128]{3,2,1,0:T(8,128)(2,1)} copy(bf16[256,8,16,128]{3,1,2,0:T(8,128)(2,1)} %bitcast.72) | data formatting | bytes 16777216
  386.6 8.8 %copy.23 = bf16[4,512,16,128]{3,1,2,0:T(8,128)(2,1)} copy(bf16[4,512,16,128]{3,2,1,0:T(8,128)(2,1)} %bitcast.69) | data formatting | bytes 16777216
  397.8 34.7 %while.15 = (s32[]{:T(128)}, f32[16,512,128]{2,1,0:T(8,128)}, f32[16,512]{1,0:T(8,128)S(1)}, f32[16,512]{1,0:T(8,128)S(1)}, s32[4]{0:T(128)S(1)}, /*index=5*/s32...) while((s32[]{:T(128)}, f32[16,512,128]{2,1,0:T(8,128)}, ...), condition=%wide.region_5.6_spmd.clone, body=%wide.region_0.5_spmd.clone.sunk | while | flops 2195997696 | bytes 66598184 | solution.py:109
  399.2 29.9 %conditional.3 = ((f32[16,512,128]{2,1,0:T(8,128)}, f32[16,512]{1,0:T(8,128)S(1)}, f32[16,512]{1,0:T(8,128)S(1)})) conditional(s32[]{:T(128)} %convert_element_type.60, (f32[16,512,128]{2,1,0:T(8,128)}, f32[16,512]{1,0:T(8,128)S(1)}, f32[16,512]{1,0:T(8,128)S(1)}) %tuple.46, (s32[]{:T(128)}, s32[]{:T(128)}, bf16[4,512,16,128]{3,1,2,0:T(8,128)(2,1)}, ...), branch_computations={%region_1.1_spmd, %region_2.4_spmd} | conditional | flops 2195997696 | bytes 66595880 | solution.py:107
  399.4 8.8 %fusion.4 = (f32[16,512]{1,0:T(8,128)S(1)}, f32[16,512,512]{2,1,0:T(8,128)}) fusion(pred[512,512]{0,1:T(8,128)(4,1)S(1)} %broadcast_compare_fusion, bf16[512,16,128]{2,0,1:T(8,128)(2,1)S(1)} %get-tuple-element.117, bf16[4,512,16,128]{3,1,2,0:T(8,128)(2,1)} %get-tuple-element.115, s32[]{:T(128)} %get-tuple-element.116), kind=kOutput, calls=%fused_computation.5 | convolution fusion | flops 1086316544 | bytes 21266944 | tf_op jit(solution)/shard_map/while/body/eval_jaxpr/cond/branch_1_fun/qhd,khd->hqk/dot_general | solution.py:86
  408.2 9.1 %fusion.2 = f32[16,512]{1,0:T(8,128)S(1)} fusion(f32[16,512,512]{2,1,0:T(8,128)} %get-tuple-element.212, f32[16,512]{1,0:T(8,128)S(1)} %max.4, pred[512,512]{0,1:T(8,128)(4,1)S(1)} %broadcast_compare_fusion), kind=kLoop, calls=%fused_computation.3 | loop fusion | flops 16769024 | bytes 17104896 | tf_op jit(solution)/shard_map/while/body/eval_jaxpr/cond/branch_1_fun/reduce_sum | solution.py:95
  417.4 11.7 %multiply_add_fusion = f32[16,512,128]{2,1,0:T(8,128)} fusion(f32[16,512,128]{2,1,0:T(8,128)} %get-tuple-element.111, f32[16,512]{1,0:T(8,128)S(1)} %get-tuple-element.210, bf16[4,512,16,128]{3,1,2,0:T(8,128)(2,1)} %get-tuple-element.118, s32[]{:T(128)} %get-tuple-element.116, f32[16,512,512]{2,1,0:T(8,128)} %get-tuple-element.212, f32[16,512]{1,0:T(8,128)S(1)} %max.4, ...), kind=kOutput, calls=%fused_computation.11 | convolution fusion | flops 1092616192 | bytes 27591168 | tf_op jit(solution)/shard_map/while/body/eval_jaxpr/cond/branch_1_fun/hqk,khd->hqd/dot_general | solution.py:96
  440.7 26.0 %fusion.25 = bf16[8192,512]{0,1:T(8,128)(2,1)} fusion(bf16[512,2048]{0,1:T(8,128)(2,1)S(1)} %bitcast.74, bf16[2048,8192]{1,0:T(8,128)(2,1)} %param.15), kind=kOutput, calls=%fused_computation.29 | convolution fusion | flops 17184063488 | bytes 44040192 | tf_op jit(solution)/shard_map/dot_general | solution.py:120
  466.8 233.4 %reduce-scatter.2.cloned.1.call-done = bf16[2048,512]{0,1:T(8,128)(2,1)} async-done(((bf16[8192,512]{0,1:T(8,128)(2,1)}), bf16[2048,512]{0,1:T(8,128)(2,1)}) %reduce-scatter.2.cloned.1.call-update) | async-done | bytes 2097168 | tf_op jit(solution)/shard_map/reduce_scatter | solution.py:119
  (58 shorter events, 80.7 us)
Async XLA Ops:
  7.2 369.6 %all-gather.2.cloned.1.call-start = ((), (), s32[]{:S(2)}) async-start(), calls=%async_computation.1 | async-start | bytes 10485760 | tf_op jit(solution)/shard_map/all_gather | solution.py:63
  8.1 19.3 %collective-permute-start = (bf16[2,3,2048]{2,0,1:T(2,128)(2,1)S(1)}, bf16[2,3,2048]{2,0,1:T(2,128)(2,1)S(1)}, u32[]{:S(2)}, u32[]{:S(2)}) collective-permute-start(bf16[2,3,2048]{2,0,1:T(2,128)(2,1)S(1)} %slice.18), channel_id=1, source_target_pairs={{0,8},{8,16},{16,24},{1,9},{9,17},{17,25},{2,10},{10,18},{18,26},{... | collective-permute-start | bytes 73736 | tf_op jit(solution)/shard_map/ppermute | solution.py:13
  72.5 17.8 %copy-start.4 = (pred[8,65]{0,1:T(8,128)(4,1)S(1)}, pred[8,65]{0,1:T(8,128)(4,1)}, u32[]{:S(2)}) copy-start(pred[8,65]{0,1:T(8,128)(4,1)} %constant.58) | copy-start | bytes 1564
  153.7 14.1 %copy-start.2 = (f32[128,2048]{1,0:T(8,128)S(1)}, f32[128,2048]{1,0:T(8,128)}, u32[]{:S(2)}) copy-start(f32[128,2048]{1,0:T(8,128)} %param.12) | copy-start | bytes 3145732
  162.4 16.4 %collective-permute-start.1 = (bf16[127,2048]{0,1:T(8,128)(2,1)}, bf16[127,2048]{0,1:T(8,128)(2,1)}, u32[]{:S(2)}, u32[]{:S(2)}) collective-permute-start(bf16[127,2048]{0,1:T(8,128)(2,1)} %slice_bitcast_fusion), channel_id=1, source_target_pairs={{0,8},{8,16},{16,24},{1,9},{9,17},{17,25},{2,10},{10,18},{18,26},{... | collective-permute-start | bytes 1560584 | tf_op jit(solution)/shard_map/ppermute | solution.py:13
  167.8 532.4 %reduce-scatter.2.cloned.1.call-start = ((), (), s32[]{:S(2)}) async-start(), calls=%async_computation.2 | async-start | bytes 10485760 | tf_op jit(solution)/shard_map/reduce_scatter | solution.py:119
  178.8 15.8 %copy-start.3 = (f32[128,2048]{1,0:T(8,128)S(1)}, f32[128,2048]{1,0:T(8,128)}, u32[]{:S(2)}) copy-start(f32[128,2048]{1,0:T(8,128)} %rev.7) | copy-start | bytes 3145732
  194.6 48.5 %copy-start = (f32[512,1,2048]{2,0,1:T(8,128)S(1)}, f32[512,1,2048]{2,0,1:T(8,128)}, u32[]{:S(2)}) copy-start(f32[512,1,2048]{2,0,1:T(8,128)} %copy.33) | copy-start | bytes 12582916
  245.5 13.5 %copy-start.1 = (bf16[512,2048]{1,0:T(8,128)(2,1)}, bf16[512,2048]{1,0:T(8,128)(2,1)S(1)}, u32[]{:S(2)}) copy-start(bf16[512,2048]{1,0:T(8,128)(2,1)S(1)} %fusion.38) | copy-start | bytes 6291460
  245.5 4.4 collective-permute-start.2
  255.1 92.9 %collective-permute-start.3 = (bf16[1024,2048]{1,0:T(8,128)(2,1)}, bf16[1024,2048]{1,0:T(8,128)(2,1)}, u32[]{:S(2)}, u32[]{:S(2)}) collective-permute-start(bf16[1024,2048]{1,0:T(8,128)(2,1)} %maximum_select_fusion.1), channel_id=1, source_target_pairs={{0,16},{8,24},{16,0},{24,8},{1,17},{9,25},{17,1},{25,9},{2,18},{10... | collective-permute-start | bytes 12582920 | tf_op jit(solution)/shard_map/ppermute | solution.py:67
Sparse Core Ops, SparseCore 0:
  167.9 58.5 all-gather.1
  466.9 233.2 reduce-scatter.1
